TPU v7x, 256 devices: a whole 4x4x8 slice. The times are simulated.
256 devices in a mesh: polar: 16 (over y, x), azimuth: 16 (over z, core).
Axes of the slice: x: 4, y: 4, z: 8, core: 2. Of those that a mesh axis runs over, the one named last changes fastest.
Arguments:
- grid_state: bfloat16 [128, 1024, 640], P('polar', 'azimuth'), may hold values from -6 to 6
- filter_taps: bfloat16 [128, 9, 4, 129], P('polar'), may hold values from -0.59765625 to 0.59765625
- support_start: int32 [128], P('polar'), may hold values from -64 to 64, as said below
- support_count: int32 [128], P('polar'), may hold values from 1 to 129
- filter_mix: bfloat16 [2, 9, 640], replicated, may hold values from -2 to 2
- w_in: bfloat16 [2, 640, 1280], replicated, may hold values from -0.25 to 0.25
- w_out: bfloat16 [2, 1280, 640], replicated, may hold values from -0.15625 to 0.15625
Outputs:
- next_state: bfloat16 [128, 1024, 640], P('polar', 'azimuth')
Inputs may be any that keep to these rules, and one draw needn't show every extreme that they name: support_start[i] + support_count[i] - 1 <= 64; support is widest near the poles.
All inputs are finite; a program needn't handle non-finite values.
Results may differ from a plain program's by a relative error of at most 0.006.
Values may be sent and summed in bfloat16 or wider, within the bound.
A program may use at most 64 MiB of HBM per device.

v0:
```python
import jax
import jax.numpy as jnp
from jax import lax
from jax.sharding import PartitionSpec as P


def from_behind(block, axis, distance):
    devices = range(lax.axis_size(axis))
    route = [(i - distance, i) for i in devices if i - distance in devices]
    return lax.ppermute(block, axis, route)


def padded(block, sides, width):
    for axis, dim in sides:
        count = lax.axis_size(axis)
        forward = [(i, i + 1) for i in range(count - 1)]
        forward.append((count - 1, 0))
        backward = [(target, source) for source, target in forward]
        low = lax.ppermute(
            lax.slice_in_dim(block, block.shape[dim] - width, None, axis=dim), axis, forward
        )
        high = lax.ppermute(lax.slice_in_dim(block, 0, width, axis=dim), axis, backward)
        block = jnp.concatenate([low, block, high], axis=dim)
    return block


def tap_bands(filter_taps, support_start, support_count, reach):
    tap_count = filter_taps.shape[-1]
    offsets = jnp.arange(tap_count, dtype=jnp.int32) - reach
    inside = (offsets[None, :] >= support_start[:, None]) & (
        offsets[None, :] < (support_start + support_count)[:, None]
    )
    masked = jnp.where(inside[:, None, None, :], filter_taps.astype(jnp.float32), jnp.float32(0.0))
    column = jnp.arange(reach, dtype=jnp.int32)[:, None]
    window = jnp.arange(3 * reach, dtype=jnp.int32)[None, :]
    onehot = (
        (window - column)[:, :, None] == jnp.arange(tap_count, dtype=jnp.int32)[None, None, :]
    ).astype(jnp.float32)
    return jnp.einsum("akrt,jwt->akjrw", masked, onehot).astype(jnp.bfloat16)


def channel_mlp(act, field, first, second):
    flat = act.reshape(-1, act.shape[-1])
    hidden = jax.nn.gelu(
        jnp.dot(flat, first, preferred_element_type=jnp.float32), approximate=False
    ).astype(jnp.bfloat16)
    update = jnp.dot(hidden, second, preferred_element_type=jnp.float32)
    return (field.astype(jnp.float32) + update.reshape(field.shape)).astype(jnp.bfloat16)


def shards(grid_state, filter_taps, support_start, support_count, filter_mix, w_in, w_out):
    lat_rows = grid_state.shape[0]
    reach = grid_state.shape[1]
    bands = tap_bands(filter_taps, support_start, support_count, reach)
    field = grid_state
    for layer_no in range(w_in.shape[0]):
        above = from_behind(field[-2:], "polar", 1)
        below = from_behind(field[:1], "polar", -1)
        extended = jnp.concatenate([above, field, below], axis=0)
        mix_row = filter_mix[layer_no].astype(jnp.float32)
        wide = padded(extended, (("azimuth", 1),), reach)
        stacked = jnp.stack([wide[lat_no : lat_no + 4] for lat_no in range(lat_rows)])
        conv = jnp.einsum("akjrw,arwc->akjc", bands, stacked, preferred_element_type=jnp.float32)
        mixed = jnp.einsum("akjc,kc->ajc", conv, mix_row)
        act = jax.nn.gelu(mixed, approximate=False).astype(jnp.bfloat16)
        field = channel_mlp(act, field, w_in[layer_no], w_out[layer_no])
    return field


def solution(mesh):
    return jax.shard_map(
        shards,
        mesh=mesh,
        in_specs=(
            P("polar", "azimuth", None),
            P("polar", None, None, None),
            P("polar"),
            P("polar"),
            P(),
            P(),
            P(),
        ),
        out_specs=P("polar", "azimuth", None),
        check_vma=False,
    )
```

profile of v0, /device:TPU:111, one launch (start us, length us, event | category | flops | bytes accessed | tf_op | source)
XLA Modules:
  0.0 132.5 jit_solution(3058758340395290741)
XLA Ops:
  0.0 1.0 slice.78
  1.0 3.1 %collective-permute-start = (bf16[2,64,640]{2,1,0:T(8,128)(2,1)S(1)}, bf16[2,64,640]{2,1,0:T(8,128)(2,1)S(1)}, u32[]{:S(2)}, u32[]{:S(2)}) collective-permute-start(bf16[2,64,640]{2,1,0:T(8,128)(2,1)S(1)} %slice.78), channel_id=1, source_target_pairs={{0,16},{16,32},{32,48},{48,64},{64,80},{80,96},{96,112},{112,128},... | collective-permute-start | bytes 491528 | tf_op jit(solution)/shard_map/ppermute | solution.py:10
  4.1 0.9 slice.79
  5.0 2.2 %collective-permute-start.1 = (bf16[1,64,640]{2,1,0:T(8,128)(2,1)S(1)}, bf16[1,64,640]{2,1,0:T(8,128)(2,1)S(1)}, u32[]{:S(2)}, u32[]{:S(2)}) collective-permute-start(bf16[1,64,640]{2,1,0:T(8,128)(2,1)S(1)} %slice.79), channel_id=1, source_target_pairs={{16,0},{32,16},{48,32},{64,48},{80,64},{96,80},{112,96},{128,112},... | collective-permute-start | bytes 245768 | tf_op jit(solution)/shard_map/ppermute | solution.py:10
  7.2 1.5 %fusion.121 = (bf16[1,9,640]{2,0,1:T(2,128)(2,1)S(1)}, bf16[1,9,640]{2,0,1:T(2,128)(2,1)}) fusion(bf16[2,9,640]{2,0,1:T(2,128)(2,1)} %param.11), kind=kLoop, calls=%fused_computation.162 | loop fusion | bytes 46080 | tf_op jit(solution)/shard_map/slice | solution.py:60
  8.6 0.6 bitcast_convert_fusion.1
  9.2 0.7 add.14
  9.9 0.7 compare_and_fusion
  10.7 1.2 constant_dynamic-update-slice_fusion.1
  11.9 0.4 collective-permute-done.1
  12.3 4.9 %collective-permute-start.2 = (bf16[11,64,640]{2,1,0:T(8,128)(2,1)S(1)}, bf16[11,64,640]{2,1,0:T(8,128)(2,1)}, u32[]{:S(2)}, u32[]{:S(2)}) collective-permute-start(bf16[11,64,640]{2,1,0:T(8,128)(2,1)S(1)} %constant_dynamic-update-slice_fusion), channel_id=1, source_target_pairs={{0,1},{1,2},{2,3},{3,4},{4,5},{5,6},{6,7},{7,8},{8,9},{9,10},{10,1... | collective-permute-start | bytes 2703368 | tf_op jit(solution)/shard_map/ppermute | solution.py:19
  17.1 0.6 iota_subtract_fusion
  17.9 5.6 %convert_bitcast_fusion = bf16[8,9,64,4,192]{4,1,3,0,2:T(8,128)(2,1)S(1)} fusion(s32[64,192]{1,0:T(8,128)} %iota_subtract_fusion, bf16[8,9,4,129]{3,2,1,0:T(4,128)(2,1)S(1)} %convert_select_fusion), kind=kOutput, calls=%fused_computation | convolution fusion | flops 914632704 | bytes 7201344 | tf_op jit(solution)/shard_map/akrt,jwt->akjrw/dot_general | solution.py:39
  23.5 3.8 %collective-permute-done.2 = bf16[11,64,640]{2,1,0:T(8,128)(2,1)} collective-permute-done((bf16[11,64,640]{2,1,0:T(8,128)(2,1)S(1)}, bf16[11,64,640]{2,1,0:T(8,128)(2,1)}, u32[]{:S(2)}, u32[]{:S(2)}) %collective-permute-start.2) | collective-permute-done | bytes 901152 | tf_op jit(solution)/shard_map/ppermute | solution.py:19
  27.3 3.8 %collective-permute-done.3 = bf16[11,64,640]{2,1,0:T(8,128)(2,1)} collective-permute-done((bf16[11,64,640]{2,1,0:T(8,128)(2,1)S(1)}, bf16[11,64,640]{2,1,0:T(8,128)(2,1)}, u32[]{:S(2)}, u32[]{:S(2)}) %collective-permute-start.3) | collective-permute-done | bytes 901152 | tf_op jit(solution)/shard_map/ppermute | solution.py:22
  31.1 1.7 %pad_maximum_fusion = bf16[11,192,640]{2,1,0:T(8,128)(2,1)S(1)} fusion(bf16[11,64,640]{2,1,0:T(8,128)(2,1)} %collective-permute-done.3, bf16[11,64,640]{2,1,0:T(8,128)(2,1)S(1)} %constant_dynamic-update-slice_fusion, bf16[11,64,640]{2,1,0:T(8,128)(2,1)} %collective-permute-done.2), kind=kLoop, calls=%fused_computation.16 | loop fusion | flops 8110080 | bytes 5406720 | tf_op jit(solution)/shard_map/concatenate | solution.py:23
  32.8 1.0 fusion.118
  33.8 1.1 fusion.117
  34.9 1.0 fusion.116
  36.0 1.0 fusion.115
  37.0 1.0 fusion.114
  38.0 1.1 fusion.113
  39.1 1.0 fusion.112
  40.1 1.0 fusion.111
  41.2 13.4 %fusion.1 = f32[640,8,64]{0,2,1:T(8,128)} fusion(f32[640,9]{0,1:T(8,128)S(1)} %copy-done.3, bf16[8,4,192,640]{3,2,1,0:T(8,128)(2,1)} %fusion.111, bf16[8,9,64,4,192]{4,1,3,0,2:T(8,128)(2,1)S(1)} %convert_bitcast_fusion), kind=kOutput, calls=%fused_computation.4 | convolution fusion | flops 4535418880 | bytes 16275968 | tf_op jit(solution)/shard_map/akjrw,arwc->akjc/dot_general | solution.py:63
  54.6 4.0 %fusion.69 = bf16[8,64,640]{2,1,0:T(8,128)(2,1)S(1)} fusion(f32[640,8,64]{0,2,1:T(8,128)} %fusion.1), kind=kLoop, calls=%fused_computation.74 | loop fusion | flops 21299200 | bytes 1966080 | tf_op jit(solution)/shard_map/convert_element_type | solution.py:65
  58.5 7.9 %fusion.13 = bf16[512,1280]{1,0:T(8,128)(2,1)S(1)} fusion(bf16[512,640]{1,0:T(8,128)(2,1)S(1)} %bitcast.272, bf16[2,640,1280]{2,1,0:T(8,128)(2,1)} %param.12), kind=kOutput, calls=%fused_computation.20 | convolution fusion | flops 881459200 | bytes 3604480 | tf_op jit(solution)/shard_map/dot_general | solution.py:45
  66.5 1.2 fusion.64
  67.7 4.0 %collective-permute-start.4 = (bf16[2,64,640]{2,1,0:T(8,128)(2,1)S(1)}, bf16[2,64,640]{2,1,0:T(8,128)(2,1)S(1)}, u32[]{:S(2)}, u32[]{:S(2)}) collective-permute-start(bf16[2,64,640]{2,1,0:T(8,128)(2,1)S(1)} %slice.112), channel_id=1, source_target_pairs={{0,16},{16,32},{32,48},{48,64},{64,80},{80,96},{96,112},{112,128},... | collective-permute-start | bytes 491528 | tf_op jit(solution)/shard_map/ppermute | solution.py:10
  71.7 1.9 %collective-permute-start.5 = (bf16[1,64,640]{2,1,0:T(8,128)(2,1)S(1)}, bf16[1,64,640]{2,1,0:T(8,128)(2,1)S(1)}, u32[]{:S(2)}, u32[]{:S(2)}) collective-permute-start(bf16[1,64,640]{2,1,0:T(8,128)(2,1)S(1)} %slice.113), channel_id=1, source_target_pairs={{16,0},{32,16},{48,32},{64,48},{80,64},{96,80},{112,96},{128,112},... | collective-permute-start | bytes 245768 | tf_op jit(solution)/shard_map/ppermute | solution.py:10
  73.6 5.4 %collective-permute-done.5 = bf16[1,64,640]{2,1,0:T(8,128)(2,1)S(1)} collective-permute-done((bf16[1,64,640]{2,1,0:T(8,128)(2,1)S(1)}, bf16[1,64,640]{2,1,0:T(8,128)(2,1)S(1)}, u32[]{:S(2)}, u32[]{:S(2)}) %collective-permute-start.5) | collective-permute-done | bytes 81952 | tf_op jit(solution)/shard_map/ppermute | solution.py:10
  79.0 0.1 pad_maximum_fusion.2
  79.1 1.4 %collective-permute-start.6 = (bf16[11,64,640]{2,1,0:T(8,128)(2,1)S(1)}, bf16[11,64,640]{2,1,0:T(8,128)(2,1)S(1)}, u32[]{:S(2)}, u32[]{:S(2)}) collective-permute-start(bf16[11,64,640]{2,1,0:T(8,128)(2,1)S(1)} %pad_maximum_fusion.2), channel_id=1, source_target_pairs={{0,1},{1,2},{2,3},{3,4},{4,5},{5,6},{6,7},{7,8},{8,9},{9,10},{10,1... | collective-permute-start | bytes 2703368 | tf_op jit(solution)/shard_map/ppermute | solution.py:19
  80.5 10.1 %collective-permute-done.6 = bf16[11,64,640]{2,1,0:T(8,128)(2,1)S(1)} collective-permute-done((bf16[11,64,640]{2,1,0:T(8,128)(2,1)S(1)}, bf16[11,64,640]{2,1,0:T(8,128)(2,1)S(1)}, u32[]{:S(2)}, u32[]{:S(2)}) %collective-permute-start.6) | collective-permute-done | bytes 901152 | tf_op jit(solution)/shard_map/ppermute | solution.py:19
  90.7 3.7 %collective-permute-done.7 = bf16[11,64,640]{2,1,0:T(8,128)(2,1)S(1)} collective-permute-done((bf16[11,64,640]{2,1,0:T(8,128)(2,1)S(1)}, bf16[11,64,640]{2,1,0:T(8,128)(2,1)S(1)}, u32[]{:S(2)}, u32[]{:S(2)}) %collective-permute-start.7) | collective-permute-done | bytes 901152 | tf_op jit(solution)/shard_map/ppermute | solution.py:22
  94.4 2.6 %pad_maximum_fusion.1 = bf16[11,192,640]{2,1,0:T(8,128)(2,1)S(1)} fusion(bf16[11,64,640]{2,1,0:T(8,128)(2,1)S(1)} %collective-permute-done.7, bf16[1,64,640]{2,1,0:T(8,128)(2,1)S(1)} %collective-permute-done.5, bf16[8,64,640]{2,1,0:T(8,128)(2,1)S(1)} %fusion.64, bf16[2,64,640]{2,1,0:T(8,128)(2,1)S(1)} %collective-permute-done.4, ...), kind=kLoop, calls=%fused_computation.17 | loop fusion | flops 13516800 | bytes 5406720 | tf_op jit(solution)/shard_map/concatenate | solution.py:23
  97.0 1.0 fusion.110
  98.0 1.1 fusion.109
  99.1 1.0 fusion.108
  100.2 1.0 fusion.107
  101.2 1.0 fusion.106
  102.2 1.1 fusion.105
  103.3 1.0 fusion.104
  104.3 1.0 fusion.103
  105.4 13.4 %fusion = f32[640,8,64]{0,2,1:T(8,128)} fusion(f32[640,9]{0,1:T(8,128)S(1)} %bitcast_convert_fusion, bf16[8,4,192,640]{3,2,1,0:T(8,128)(2,1)} %fusion.103, bf16[8,9,64,4,192]{4,1,3,0,2:T(8,128)(2,1)S(1)} %convert_bitcast_fusion), kind=kOutput, calls=%fused_computation.2 | convolution fusion | flops 4535418880 | bytes 16275968 | tf_op jit(solution)/shard_map/akjrw,arwc->akjc/dot_general | solution.py:63
  118.7 4.0 %fusion.72 = bf16[8,64,640]{2,1,0:T(8,128)(2,1)S(1)} fusion(f32[640,8,64]{0,2,1:T(8,128)} %fusion), kind=kLoop, calls=%fused_computation.77 | loop fusion | flops 21299200 | bytes 1966080 | tf_op jit(solution)/shard_map/convert_element_type | solution.py:65
  122.7 7.7 %fusion.16 = bf16[512,1280]{1,0:T(8,128)(2,1)S(1)} fusion(bf16[512,640]{1,0:T(8,128)(2,1)S(1)} %bitcast.273, bf16[2,640,1280]{2,1,0:T(8,128)(2,1)} %param.12), kind=kOutput, calls=%fused_computation.23 | convolution fusion | flops 881459200 | bytes 3604480 | tf_op jit(solution)/shard_map/dot_general | solution.py:45
  130.4 2.0 %fusion.61 = bf16[8,64,640]{2,1,0:T(8,128)(2,1)} fusion(bf16[8,64,1280]{2,1,0:T(8,128)(2,1)S(1)} %bitcast.274, bf16[2,1280,640]{2,1,0:T(8,128)(2,1)S(1)} %copy-done.5, bf16[8,64,640]{2,1,0:T(8,128)(2,1)S(1)} %fusion.64), kind=kOutput, calls=%fused_computation.70 | convolution fusion | flops 839843840 | bytes 4259840 | tf_op jit(solution)/shard_map/dot_general | solution.py:47
  (23 shorter events, 0.2 us)
Async XLA Ops:
  0.0 17.8 %copy-start.1 = (bf16[8,9,4,129]{3,2,1,0:T(4,128)(2,1)S(1)}, bf16[8,9,4,129]{3,2,1,0:T(4,128)(2,1)}, u32[]{:S(2)}) copy-start(bf16[8,9,4,129]{3,2,1,0:T(4,128)(2,1)} %param.8) | copy-start | bytes 222916
  1.0 9.7 %collective-permute-start = (bf16[2,64,640]{2,1,0:T(8,128)(2,1)S(1)}, bf16[2,64,640]{2,1,0:T(8,128)(2,1)S(1)}, u32[]{:S(2)}, u32[]{:S(2)}) collective-permute-start(bf16[2,64,640]{2,1,0:T(8,128)(2,1)S(1)} %slice.78), channel_id=1, source_target_pairs={{0,16},{16,32},{32,48},{48,64},{64,80},{80,96},{96,112},{112,128},... | collective-permute-start | bytes 491528 | tf_op jit(solution)/shard_map/ppermute | solution.py:10
  5.0 7.3 %collective-permute-start.1 = (bf16[1,64,640]{2,1,0:T(8,128)(2,1)S(1)}, bf16[1,64,640]{2,1,0:T(8,128)(2,1)S(1)}, u32[]{:S(2)}, u32[]{:S(2)}) collective-permute-start(bf16[1,64,640]{2,1,0:T(8,128)(2,1)S(1)} %slice.79), channel_id=1, source_target_pairs={{16,0},{32,16},{48,32},{64,48},{80,64},{96,80},{112,96},{128,112},... | collective-permute-start | bytes 245768 | tf_op jit(solution)/shard_map/ppermute | solution.py:10
  12.3 15.0 %collective-permute-start.2 = (bf16[11,64,640]{2,1,0:T(8,128)(2,1)S(1)}, bf16[11,64,640]{2,1,0:T(8,128)(2,1)}, u32[]{:S(2)}, u32[]{:S(2)}) collective-permute-start(bf16[11,64,640]{2,1,0:T(8,128)(2,1)S(1)} %constant_dynamic-update-slice_fusion), channel_id=1, source_target_pairs={{0,1},{1,2},{2,3},{3,4},{4,5},{5,6},{6,7},{7,8},{8,9},{9,10},{10,1... | collective-permute-start | bytes 2703368 | tf_op jit(solution)/shard_map/ppermute | solution.py:19
  17.1 14.0 %collective-permute-start.3 = (bf16[11,64,640]{2,1,0:T(8,128)(2,1)S(1)}, bf16[11,64,640]{2,1,0:T(8,128)(2,1)}, u32[]{:S(2)}, u32[]{:S(2)}) collective-permute-start(bf16[11,64,640]{2,1,0:T(8,128)(2,1)S(1)} %constant_dynamic-update-slice_fusion), channel_id=1, source_target_pairs={{1,0},{2,1},{3,2},{4,3},{5,4},{6,5},{7,6},{8,7},{9,8},{10,9},{11,1... | collective-permute-start | bytes 2703368 | tf_op jit(solution)/shard_map/ppermute | solution.py:22
  38.0 3.1 %copy-start.3 = (f32[640,9]{0,1:T(8,128)S(1)}, f32[640,9]{0,1:T(8,128)}, u32[]{:S(2)}) copy-start(f32[640,9]{0,1:T(8,128)} %bitcast_convert_fusion.1) | copy-start | bytes 69124
  58.5 7.9 %copy-start = (bf16[8,64,640]{2,1,0:T(8,128)(2,1)S(1)}, bf16[8,64,640]{2,1,0:T(8,128)(2,1)}, u32[]{:S(2)}) copy-start(bf16[8,64,640]{2,1,0:T(8,128)(2,1)} %param.7) | copy-start | bytes 1966084
  58.5 7.9 %copy-start.4 = (bf16[2,1280,640]{2,1,0:T(8,128)(2,1)S(1)}, bf16[2,1280,640]{2,1,0:T(8,128)(2,1)}, u32[]{:S(2)}) copy-start(bf16[2,1280,640]{2,1,0:T(8,128)(2,1)} %param.13) | copy-start | bytes 9830404
  66.5 14.1 %copy-start.2 = (bf16[1,9,640]{2,0,1:T(2,128)(2,1)S(1)}, bf16[1,9,640]{2,0,1:T(2,128)(2,1)}, u32[]{:S(2)}) copy-start(bf16[1,9,640]{2,0,1:T(2,128)(2,1)} %get-tuple-element.6) | copy-start | bytes 34564
  67.7 11.3 %collective-permute-start.4 = (bf16[2,64,640]{2,1,0:T(8,128)(2,1)S(1)}, bf16[2,64,640]{2,1,0:T(8,128)(2,1)S(1)}, u32[]{:S(2)}, u32[]{:S(2)}) collective-permute-start(bf16[2,64,640]{2,1,0:T(8,128)(2,1)S(1)} %slice.112), channel_id=1, source_target_pairs={{0,16},{16,32},{32,48},{48,64},{64,80},{80,96},{96,112},{112,128},... | collective-permute-start | bytes 491528 | tf_op jit(solution)/shard_map/ppermute | solution.py:10
  71.7 7.3 %collective-permute-start.5 = (bf16[1,64,640]{2,1,0:T(8,128)(2,1)S(1)}, bf16[1,64,640]{2,1,0:T(8,128)(2,1)S(1)}, u32[]{:S(2)}, u32[]{:S(2)}) collective-permute-start(bf16[1,64,640]{2,1,0:T(8,128)(2,1)S(1)} %slice.113), channel_id=1, source_target_pairs={{16,0},{32,16},{48,32},{64,48},{80,64},{96,80},{112,96},{128,112},... | collective-permute-start | bytes 245768 | tf_op jit(solution)/shard_map/ppermute | solution.py:10
  79.1 11.6 %collective-permute-start.6 = (bf16[11,64,640]{2,1,0:T(8,128)(2,1)S(1)}, bf16[11,64,640]{2,1,0:T(8,128)(2,1)S(1)}, u32[]{:S(2)}, u32[]{:S(2)}) collective-permute-start(bf16[11,64,640]{2,1,0:T(8,128)(2,1)S(1)} %pad_maximum_fusion.2), channel_id=1, source_target_pairs={{0,1},{1,2},{2,3},{3,4},{4,5},{5,6},{6,7},{7,8},{8,9},{9,10},{10,1... | collective-permute-start | bytes 2703368 | tf_op jit(solution)/shard_map/ppermute | solution.py:19
  80.5 13.9 %collective-permute-start.7 = (bf16[11,64,640]{2,1,0:T(8,128)(2,1)S(1)}, bf16[11,64,640]{2,1,0:T(8,128)(2,1)S(1)}, u32[]{:S(2)}, u32[]{:S(2)}) collective-permute-start(bf16[11,64,640]{2,1,0:T(8,128)(2,1)S(1)} %pad_maximum_fusion.2), channel_id=1, source_target_pairs={{1,0},{2,1},{3,2},{4,3},{5,4},{6,5},{7,6},{8,7},{9,8},{10,9},{11,1... | collective-permute-start | bytes 2703368 | tf_op jit(solution)/shard_map/ppermute | solution.py:22
  122.7 7.7 %copy-start.5 = (bf16[2,1280,640]{2,1,0:T(8,128)(2,1)S(1)}, bf16[2,1280,640]{2,1,0:T(8,128)(2,1)}, u32[]{:S(2)}) copy-start(bf16[2,1280,640]{2,1,0:T(8,128)(2,1)} %param.13) | copy-start | bytes 9830404
where the time goes:
time: 133 us; the launch traced here: 132 us
  matrix products  51.1 us (38%)
  waiting for transfers between devices  27.3 us (21%)
  local copies, waits for them, and re-layouts  21.4 us (16%)
  starting transfers between devices  17.4 us (13%)
  other arithmetic  15 us (11%)
    dot_general x2, matrix products, shards(): jnp.einsum('akjrw,arwc->akjc', bands, stacked, preferred_element_type=jnp...  26.7 us
    unnamed x28, local copies, waits for them, and re-layouts  15.9 us
    dot_general x2, matrix products, channel_mlp(): jnp.dot(flat, first, preferred_element_type=jnp.float32)  15.6 us
    ppermute x2, waiting for transfers between devices, padded(): lax.ppermute(lax.slice_in_dim(block, block.shape[dim] - width, None, axis...  14 us
    ppermute x4, starting transfers between devices, from_behind(): return lax.ppermute(block, axis, route)  11.1 us
    convert_element_type x2, other arithmetic, shards(): act = jax.nn.gelu(mixed, approximate=False).astype(jnp.bfloat16)  7.9 us
    ppermute x2, waiting for transfers between devices, padded(): lax.ppermute(lax.slice_in_dim(block, 0, width, axis=dim), axis, backward)  7.49 us
    ppermute x2, starting transfers between devices, padded(): lax.ppermute(lax.slice_in_dim(block, block.shape[dim] - width, None, axis...  6.3 us
  transfers between devices with their start and end apart: 8, of which 6 were waited for; matrix products, arithmetic and copies ran while one was open for 9% of the time, Pallas kernels for 0%

commit v1 on v0

v1 whole, which is shorter than its diff:
```python
import functools

import jax
import jax.numpy as jnp
from jax import lax
from jax.experimental import pallas as pl
from jax.experimental.pallas import tpu as pltpu
from jax.sharding import PartitionSpec as P

F32 = jnp.float32
BF16 = jnp.bfloat16
MESH = pl.DeviceIdType.MESH
CHUNKS = ((0, 256), (256, 256), (512, 128))
NAMES = (
    "z6", "z0", "z4", "z1", "pairA", "pairB",
    "down", "up", "sdown", "sup", "fdown", "fup",
)


def gelu(x):
    return 0.5 * x * (1.0 + lax.erf(x * 0.7071067811865476))


def body(
    n_polar, n_azimuth,
    grid, taps, start, count, mix, w_in, w_out, out,
    f1, fz, ab, cc, w1, w2, src, mab, mcc, part, act, mixf,
    send_sem, recv_sem, local_sem,
):
    p = lax.axis_index("polar")
    a = lax.axis_index("azimuth")
    h = lax.rem(a, 2)
    pair = a + 1 - 2 * h
    zside = lax.rem(a + n_azimuth - 1 + 2 * h, n_azimuth)
    has_low = p > 0
    has_high = p < n_polar - 1
    own = pl.ds(pl.multiple_of(h * 64, 64), 64)

    barrier = pltpu.get_barrier_semaphore()
    for peer in (pair, zside):
        pl.semaphore_signal(barrier, inc=1, device_id=(p, peer), device_id_type=MESH)

    @pl.when(has_low)
    def _():
        pl.semaphore_signal(barrier, inc=1, device_id=(p - 1, a), device_id_type=MESH)

    @pl.when(has_high)
    def _():
        pl.semaphore_signal(barrier, inc=1, device_id=(p + 1, a), device_id_type=MESH)

    def field_rows(layer, row, rows):
        if layer == 0:
            return grid.at[pl.ds(row, rows)]
        return f1.at[layer, pl.ds(row + 2, rows), own]

    def transfer(layer, name):
        up_p, down_p = p + 1, p - 1
        if name[0] == "z":
            row = int(name[1])
            rows = 3 if row == 1 else (1 if row == 0 else 2)
            return (field_rows(layer, row, rows), fz.at[layer, pl.ds(row + 2, rows)], (p, zside), None, None)
        if name[:4] == "pair":
            row = 4 if name == "pairA" else 0
            return (field_rows(layer, row, 4), f1.at[layer, pl.ds(row + 2, 4), own], (p, pair), None, None)
        if name == "down":
            return (field_rows(layer, 6, 2), f1.at[layer, pl.ds(0, 2), own], (up_p, a), has_high, has_low)
        if name == "up":
            return (field_rows(layer, 0, 1), f1.at[layer, pl.ds(10, 1), own], (down_p, a), has_low, has_high)
        if name == "sdown":
            return (fz.at[layer, pl.ds(8, 2)], fz.at[layer, pl.ds(0, 2)], (up_p, a), has_high, has_low)
        if name == "sup":
            return (fz.at[layer, pl.ds(2, 1)], fz.at[layer, pl.ds(10, 1)], (down_p, a), has_low, has_high)
        if name == "fdown":
            return (f1.at[layer, pl.ds(0, 2), own], f1.at[layer, pl.ds(0, 2), own], (p, pair), has_low, has_low)
        return (f1.at[layer, pl.ds(10, 1), own], f1.at[layer, pl.ds(10, 1), own], (p, pair), has_high, has_high)

    def act_on(layer, name, what):
        source, target, device, sends, receives = transfer(layer, name)
        number = layer * len(NAMES) + NAMES.index(name)
        copy = pltpu.make_async_remote_copy(
            src_ref=source, dst_ref=target, send_sem=send_sem.at[number],
            recv_sem=recv_sem.at[number], device_id=device, device_id_type=MESH,
        )
        run = {"start": copy.start, "recv": copy.wait_recv, "sent": copy.wait_send}[what]
        when = receives if what == "recv" else sends
        if when is None:
            run()
        else:
            pl.when(when)(run)

    def begin(layer, *names):
        for name in names:
            act_on(layer, name, "start")

    def arrived(layer, *names):
        for name in names:
            act_on(layer, name, "recv")

    local = [
        pltpu.make_async_copy(grid, f1.at[0, pl.ds(2, 8), own], local_sem.at[0]),
        pltpu.make_async_copy(w_in.at[0], w1.at[0], local_sem.at[1]),
        pltpu.make_async_copy(w_out.at[0], w2.at[0], local_sem.at[2]),
        pltpu.make_async_copy(w_in.at[1], w1.at[1], local_sem.at[3]),
        pltpu.make_async_copy(w_out.at[1], w2.at[1], local_sem.at[4]),
    ]
    local[0].start()

    pl.semaphore_wait(barrier, 2 + has_low.astype(jnp.int32) + has_high.astype(jnp.int32))

    begin(0, "z6", "down", "pairA", "up", "z0", "pairB", "z4", "z1")
    for copy in local[1:]:
        copy.start()

    @pl.when(p == 0)
    def _():
        for layer in range(2):
            f1[layer, 0:2] = jnp.zeros((2, 128, 640), BF16)
            fz[layer, 0:2] = jnp.zeros((2, 64, 640), BF16)

    @pl.when(p == n_polar - 1)
    def _():
        for layer in range(2):
            f1[layer, 10:11] = jnp.zeros((1, 128, 640), BF16)
            fz[layer, 10:11] = jnp.zeros((1, 64, 640), BF16)

    for layer in range(2):
        mixf[layer, 0:9] = mix[layer].astype(F32)

    row64 = lax.broadcasted_iota(jnp.int32, (64, 128), 0)
    lane64 = lax.broadcasted_iota(jnp.int32, (64, 128), 1)
    tap_ab = 64 * (1 - h) + lane64 - row64
    mab[...] = jnp.where((tap_ab >= 0) & (tap_ab <= 128), 1.0, 0.0).astype(F32)
    tap_cc = 128 * h + (lane64 & 63) - row64
    mcc[...] = jnp.where((tap_cc >= 0) & (tap_cc <= 128), 1.0, 0.0).astype(F32)

    offset = lax.broadcasted_iota(jnp.int32, (4, 129), 1) - 64
    lane4 = lax.broadcasted_iota(jnp.int32, (4, 128), 1)
    first = lane4 == 0
    even = ((h == 0) & (lane4 < 64)) | ((h == 1) & (first | (lane4 > 64)))

    def sources(n, carry):
        i, k = n // 9, lax.rem(n, 9)
        inside = (offset >= start[i]) & (offset < start[i] + count[i])
        v = jnp.where(inside, taps[i, k].astype(F32), 0.0)
        low = v[:, 0:128]
        last = jnp.where(first, jnp.broadcast_to(v[:, 128:129], (4, 128)), low)
        v_ab = jnp.where(h == 0, pltpu.roll(last, 64, 1), low)
        v_cc = jnp.where(h == 0, low, last)
        other = pltpu.roll(v_cc, 64, 1)
        odd = jnp.concatenate([other[1:4], other[0:1]], axis=0)
        src[n, 0:4] = v_ab
        src[n, 4:8] = jnp.where(even, v_cc, odd)
        return carry

    lax.fori_loop(0, 72, sources, 0)

    def band(n, row, mask):
        base = jnp.broadcast_to(src[n, row : row + 1, :], (8, 128))
        base = pltpu.roll(base, 0, 1, stride=1, stride_axis=0)
        tiles = [base] + [pltpu.roll(base, 8 * j, 1) for j in range(1, 8)]
        return (jnp.concatenate(tiles, axis=0) * mask[...]).astype(BF16)

    def build(n, carry):
        i, k = n // 9, lax.rem(n, 9)
        rows = pl.ds(pl.multiple_of(k * 64, 64), 64)
        for r in range(4):
            ab[i, rows, 128 * r : 128 * r + 128] = band(n, r, mab)
        for r in range(2):
            cc[i, rows, 128 * r : 128 * r + 128] = band(n, 4 + 2 * r, mcc)
        return carry

    lax.fori_loop(0, 72, build, 0)

    def mixed(layer, r, c0, cw):
        total = r[0:64] * mixf[layer, 0:1, c0 : c0 + cw]
        for k in range(1, 9):
            total += r[64 * k : 64 * k + 64] * mixf[layer, k : k + 1, c0 : c0 + cw]
        return total

    def near(layer, lo, hi):
        def one(i, carry):
            rows = pl.ds(pl.multiple_of(i * 64, 64), 64)
            for c0, cw in CHUNKS:
                window = f1[layer, pl.ds(i, 4), :, c0 : c0 + cw].reshape(512, cw)
                r = jnp.dot(ab[i], window, preferred_element_type=F32)
                part[rows, c0 : c0 + cw] = mixed(layer, r, c0, cw)
            return carry

        lax.fori_loop(lo, hi, one, 0)

    def far(layer, lo, hi):
        def one(i, carry):
            rows = pl.ds(pl.multiple_of(i * 64, 64), 64)
            for c0, cw in CHUNKS:
                window = fz[layer, pl.ds(i, 4), :, c0 : c0 + cw].reshape(256, cw)
                r = jnp.dot(cc[i], window, preferred_element_type=F32)
                total = part[rows, c0 : c0 + cw] + mixed(layer, r, c0, cw)
                act[rows, c0 : c0 + cw] = gelu(total).astype(BF16)
            return carry

        lax.fori_loop(lo, hi, one, 0)

    def mlp(layer, row):
        hidden = jnp.dot(act[row * 64 : row * 64 + 256], w1[layer], preferred_element_type=F32)
        hidden = gelu(hidden).astype(BF16)
        update = jnp.dot(hidden, w2[layer], preferred_element_type=F32)
        field = f1[layer, row + 2 : row + 6, own, :].astype(F32)
        result = (field + update.reshape(4, 64, 640)).astype(BF16)
        if layer == 0:
            f1[1, row + 2 : row + 6, own, :] = result
        else:
            out[row : row + 4] = result

    arrived(0, "z6", "z0")
    begin(0, "sdown", "sup")
    local[0].wait()
    arrived(0, "pairA", "pairB")
    near(0, 4, 7)
    arrived(0, "down", "up")
    begin(0, "fdown", "fup")
    near(0, 2, 4)
    arrived(0, "fdown", "fup")
    near(0, 7, 8)
    near(0, 0, 2)
    arrived(0, "z4", "z1")
    far(0, 4, 7)
    arrived(0, "sup")
    far(0, 7, 8)
    local[1].wait()
    local[2].wait()
    mlp(0, 4)
    begin(1, "z6", "down", "pairA", "z4")
    far(0, 2, 4)
    arrived(0, "sdown")
    far(0, 0, 2)
    mlp(0, 0)
    begin(1, "z0", "up", "pairB", "z1")

    arrived(1, "z6")
    begin(1, "sdown")
    arrived(1, "pairA", "pairB")
    near(1, 2, 4)
    arrived(1, "down")
    begin(1, "fdown")
    arrived(1, "z0")
    begin(1, "sup")
    near(1, 4, 7)
    arrived(1, "up")
    begin(1, "fup")
    arrived(1, "fdown")
    near(1, 0, 2)
    arrived(1, "fup")
    near(1, 7, 8)
    arrived(1, "z4", "z1")
    far(1, 4, 7)
    arrived(1, "sup")
    far(1, 7, 8)
    local[3].wait()
    local[4].wait()
    mlp(1, 4)
    far(1, 2, 4)
    arrived(1, "sdown")
    far(1, 0, 2)
    mlp(1, 0)

    for layer in range(2):
        for name in NAMES:
            act_on(layer, name, "sent")


def shards(n_polar, n_azimuth, grid, taps, start, count, mix, w_in, w_out):
    copies = 2 * len(NAMES)
    vmem = pl.BlockSpec(memory_space=pltpu.VMEM)
    smem = pl.BlockSpec(memory_space=pltpu.SMEM)
    hbm = pl.BlockSpec(memory_space=pl.ANY)
    return pl.pallas_call(
        functools.partial(body, n_polar, n_azimuth),
        out_shape=jax.ShapeDtypeStruct(grid.shape, grid.dtype),
        in_specs=[hbm, vmem, smem, smem, vmem, hbm, hbm],
        out_specs=vmem,
        scratch_shapes=[
            pltpu.VMEM((2, 11, 128, 640), BF16),
            pltpu.VMEM((2, 11, 64, 640), BF16),
            pltpu.VMEM((8, 576, 512), BF16),
            pltpu.VMEM((8, 576, 256), BF16),
            pltpu.VMEM((2, 640, 1280), BF16),
            pltpu.VMEM((2, 1280, 640), BF16),
            pltpu.VMEM((72, 8, 128), F32),
            pltpu.VMEM((64, 128), F32),
            pltpu.VMEM((64, 128), F32),
            pltpu.VMEM((512, 640), F32),
            pltpu.VMEM((512, 640), BF16),
            pltpu.VMEM((2, 16, 640), F32),
            pltpu.SemaphoreType.DMA((copies,)),
            pltpu.SemaphoreType.DMA((copies,)),
            pltpu.SemaphoreType.DMA((5,)),
        ],
        compiler_params=pltpu.CompilerParams(
            collective_id=0, has_side_effects=True, vmem_limit_bytes=48 * 2**20
        ),
    )(grid, taps, start, count, mix, w_in, w_out)


def solution(mesh):
    return jax.shard_map(
        functools.partial(shards, mesh.shape["polar"], mesh.shape["azimuth"]),
        mesh=mesh,
        in_specs=(
            P("polar", "azimuth", None),
            P("polar", None, None, None),
            P("polar"),
            P("polar"),
            P(),
            P(),
            P(),
        ),
        out_specs=P("polar", "azimuth", None),
        check_vma=False,
    )
```

time: 133 us -> 64.3 us (0.48)
  the two profiles are of different devices: /device:TPU:111 before, /device:TPU:24 now
where the time goes in v1:
time: 64.3 us; the launch traced here: 63.8 us
  Pallas kernels  57 us (89%)
  local copies, waits for them, and re-layouts  6.81 us (11%)
    pallas_call x1, Pallas kernels, shards(): pl.pallas_call(functools.partial(body, n_polar, n_azimuth), out_shape=jax...  57 us
    unnamed x12, local copies, waits for them, and re-layouts  6.81 us

profile of v1, /device:TPU:24, one launch (start us, length us, event | category | flops | bytes accessed | tf_op | source)
XLA Modules:
  0.0 63.8 jit_solution(4246561431877712236)
XLA Ops:
  0.0 0.7 %copy.8.mix = bf16[2,9,640]{2,1,0:T(8,128)(2,1)S(1)} copy(bf16[2,9,640]{2,0,1:T(2,128)(2,1)} %param.11) | data formatting | bytes 46080 | tf_op args[4]
  0.7 0.0 copy-start
  0.7 1.9 %copy-done = bf16[2,640,1280]{2,1,0:T(8,128)(2,1)S(1)} copy-done((bf16[2,640,1280]{2,1,0:T(8,128)(2,1)S(1)}, bf16[2,640,1280]{2,1,0:T(8,128)(2,1)}, u32[]{:S(2)}) %copy-start) | copy-done | bytes 3276824
  2.7 0.0 copy-start.1
  2.7 1.1 %copy-done.1 = bf16[8,64,640]{2,1,0:T(8,128)(2,1)S(1)} copy-done((bf16[8,64,640]{2,1,0:T(8,128)(2,1)S(1)}, bf16[8,64,640]{2,1,0:T(8,128)(2,1)}, u32[]{:S(2)}) %copy-start.1) | copy-done | bytes 655384
  3.8 0.0 copy-start.2
  3.8 0.9 %copy-done.2 = bf16[8,9,4,129]{3,2,1,0:T(4,128)(2,1)S(1)} copy-done((bf16[8,9,4,129]{3,2,1,0:T(4,128)(2,1)S(1)}, bf16[8,9,4,129]{3,2,1,0:T(4,128)(2,1)}, u32[]{:S(2)}) %copy-start.2) | copy-done | bytes 74328
  4.7 0.0 copy-start.3
  4.7 0.7 %copy-done.3 = s32[8]{0:T(128)S(1)} copy-done((s32[8]{0:T(128)S(1)}, s32[8]{0:T(128)}, u32[]{:S(2)}) %copy-start.3) | copy-done | bytes 56
  5.3 0.0 copy-start.4
  5.3 0.7 %copy-done.4 = s32[8]{0:T(128)S(1)} copy-done((s32[8]{0:T(128)S(1)}, s32[8]{0:T(128)}, u32[]{:S(2)}) %copy-start.4) | copy-done | bytes 56
  6.0 57.0 %shard_map.73 = bf16[8,64,640]{2,1,0:T(8,128)(2,1)S(1)} custom-call(bf16[8,64,640]{2,1,0:T(8,128)(2,1)S(1)} %copy-done.1, bf16[8,9,4,129]{3,2,1,0:T(4,128)(2,1)S(1)} %copy-done.2, s32[8]{0:T(128)S(1)} %copy-done.3, s32[8]{0:T(128)S(1)} %copy-done.4, bf16[2,9,640]{2,1,0:T(8,128)(2,1)S(1)} %copy.8.mix, bf16[2,640,1280]{2,1,0:T(8,128)(2,1)S(1)} %copy-done, ...), custom_call_target="tpu_custom_call" | custom-call | tf_op jit(solution)/shard_map/pallas_call | solution.py:276
  63.0 0.8 %copy.10 = bf16[8,64,640]{2,1,0:T(8,128)(2,1)} copy(bf16[8,64,640]{2,1,0:T(8,128)(2,1)S(1)} %shard_map.73) | data formatting | bytes 1310720
Async XLA Ops:
  0.7 1.9 %copy-start = (bf16[2,640,1280]{2,1,0:T(8,128)(2,1)S(1)}, bf16[2,640,1280]{2,1,0:T(8,128)(2,1)}, u32[]{:S(2)}) copy-start(bf16[2,640,1280]{2,1,0:T(8,128)(2,1)} %w_in.1) | copy-start | bytes 9830404
  2.7 1.1 %copy-start.1 = (bf16[8,64,640]{2,1,0:T(8,128)(2,1)S(1)}, bf16[8,64,640]{2,1,0:T(8,128)(2,1)}, u32[]{:S(2)}) copy-start(bf16[8,64,640]{2,1,0:T(8,128)(2,1)} %grid.1) | copy-start | bytes 1966084
  3.8 0.9 %copy-start.2 = (bf16[8,9,4,129]{3,2,1,0:T(4,128)(2,1)S(1)}, bf16[8,9,4,129]{3,2,1,0:T(4,128)(2,1)}, u32[]{:S(2)}) copy-start(bf16[8,9,4,129]{3,2,1,0:T(4,128)(2,1)} %taps.1) | copy-start | bytes 222916
  4.7 0.7 %copy-start.3 = (s32[8]{0:T(128)S(1)}, s32[8]{0:T(128)}, u32[]{:S(2)}) copy-start(s32[8]{0:T(128)} %start.1) | copy-start | bytes 100
  5.3 0.7 %copy-start.4 = (s32[8]{0:T(128)S(1)}, s32[8]{0:T(128)}, u32[]{:S(2)}) copy-start(s32[8]{0:T(128)} %count.1) | copy-start | bytes 100

commit v2 on v1

v2 whole, which is shorter than its diff:
```python
import functools

import jax
import jax.numpy as jnp
from jax import lax
from jax.experimental import pallas as pl
from jax.experimental.pallas import tpu as pltpu
from jax.sharding import PartitionSpec as P

F32 = jnp.float32
BF16 = jnp.bfloat16
MESH = pl.DeviceIdType.MESH
NAMES = (
    "z0", "z2", "z4", "z6", "p0", "p2", "p4", "p6",
    "down", "up", "sdown", "sup", "fdown", "fup",
)


def gelu(x):
    return 0.5 * x * (1.0 + lax.erf(x * 0.7071067811865476))


def body(
    n_polar, n_azimuth,
    grid, taps_in, start_in, count_in, mix_in, w_in, w_out, out,
    f, band, w1, w2, taps, start, count, mix, src, act, mixf,
    send_sem, recv_sem, local_sem,
):
    p = lax.axis_index("polar")
    a = lax.axis_index("azimuth")
    h = lax.rem(a, 2)
    pair = a + 1 - 2 * h
    zside = lax.rem(a + n_azimuth - 1 + 2 * h, n_azimuth)
    has_low = p > 0
    has_high = p < n_polar - 1
    own = pl.ds(64, 64)
    core_side = pl.ds(pl.multiple_of(128 * (1 - h), 128), 64)
    chip_side = pl.ds(pl.multiple_of(128 * h, 128), 64)

    barrier = pltpu.get_barrier_semaphore()
    for peer in (pair, zside):
        pl.semaphore_signal(barrier, inc=1, device_id=(p, peer), device_id_type=MESH)

    @pl.when(has_low)
    def _():
        pl.semaphore_signal(barrier, inc=1, device_id=(p - 1, a), device_id_type=MESH)

    @pl.when(has_high)
    def _():
        pl.semaphore_signal(barrier, inc=1, device_id=(p + 1, a), device_id_type=MESH)

    def field_rows(layer, row, rows):
        if layer == 0:
            return grid.at[pl.ds(row, rows)]
        return f.at[layer, pl.ds(row + 2, rows), own]

    def transfer(layer, name):
        if name[0] == "z":
            row = int(name[1])
            return (field_rows(layer, row, 2), f.at[layer, pl.ds(row + 2, 2), core_side], (p, zside), None, None)
        if name[0] == "p":
            row = int(name[1])
            return (field_rows(layer, row, 2), f.at[layer, pl.ds(row + 2, 2), chip_side], (p, pair), None, None)
        if name == "down":
            return (field_rows(layer, 6, 2), f.at[layer, pl.ds(0, 2), own], (p + 1, a), has_high, has_low)
        if name == "up":
            return (field_rows(layer, 0, 1), f.at[layer, pl.ds(10, 1), own], (p - 1, a), has_low, has_high)
        if name == "sdown":
            return (f.at[layer, pl.ds(8, 2), chip_side], f.at[layer, pl.ds(0, 2), chip_side], (p + 1, a), has_high, has_low)
        if name == "sup":
            return (f.at[layer, pl.ds(2, 1), chip_side], f.at[layer, pl.ds(10, 1), chip_side], (p - 1, a), has_low, has_high)
        if name == "fdown":
            return (f.at[layer, pl.ds(0, 2), own], f.at[layer, pl.ds(0, 2), chip_side], (p, pair), has_low, has_low)
        return (f.at[layer, pl.ds(10, 1), own], f.at[layer, pl.ds(10, 1), chip_side], (p, pair), has_high, has_high)

    def act_on(layer, name, what):
        source, target, device, sends, receives = transfer(layer, name)
        number = layer * len(NAMES) + NAMES.index(name)
        copy = pltpu.make_async_remote_copy(
            src_ref=source, dst_ref=target, send_sem=send_sem.at[number],
            recv_sem=recv_sem.at[number], device_id=device, device_id_type=MESH,
        )
        run = {"start": copy.start, "recv": copy.wait_recv, "sent": copy.wait_send}[what]
        when = receives if what == "recv" else sends
        if when is None:
            run()
        else:
            pl.when(when)(run)

    def begin(layer, *names):
        for name in names:
            act_on(layer, name, "start")

    def arrived(layer, *names):
        for name in names:
            act_on(layer, name, "recv")

    local = {
        name: pltpu.make_async_copy(source, target, local_sem.at[number])
        for number, (name, source, target) in enumerate((
            ("taps", taps_in, taps),
            ("start", start_in, start),
            ("count", count_in, count),
            ("mix", mix_in, mix),
            ("field", grid, f.at[0, pl.ds(2, 8), own]),
            ("in0", w_in.at[0], w1.at[0]),
            ("out0", w_out.at[0], w2.at[0]),
            ("in1", w_in.at[1], w1.at[1]),
            ("out1", w_out.at[1], w2.at[1]),
        ))
    }
    for copy in local.values():
        copy.start()

    pl.semaphore_wait(barrier, 2 + has_low.astype(jnp.int32) + has_high.astype(jnp.int32))

    begin(0, "z0", "down", "up", "p0", "z2", "p2", "z4", "p4", "z6", "p6")

    @pl.when(p == 0)
    def _():
        for layer in range(2):
            f[layer, 0:2] = jnp.zeros((2, 192, 640), BF16)

    @pl.when(p == n_polar - 1)
    def _():
        for layer in range(2):
            f[layer, 10:11] = jnp.zeros((1, 192, 640), BF16)

    for name in ("taps", "start", "count", "mix"):
        local[name].wait()
    for layer in range(2):
        for k in range(9):
            mixf[layer, k : k + 1] = mix[k, layer : layer + 1].astype(F32)

    offset = lax.broadcasted_iota(jnp.int32, (4, 129), 1) - 64
    lane4 = lax.broadcasted_iota(jnp.int32, (4, 128), 1)
    row4 = lax.broadcasted_iota(jnp.int32, (4, 128), 0)
    lane32 = lax.broadcasted_iota(jnp.int32, (32, 128), 1)
    row32 = lax.broadcasted_iota(jnp.int32, (32, 128), 0)
    ends = ((lane4 + 127 - 32 * row4) & 127) >= 96

    def sources(i, carry):
        inside = (offset >= start[i]) & (offset < start[i] + count[i])
        for k in range(9):
            v = jnp.where(inside, taps[i, k].astype(F32), 0.0)
            low = v[:, 0:128]
            last = jnp.where(lane4 == 0, jnp.broadcast_to(v[:, 128:129], (4, 128)), low)
            tail = last
            for r in range(1, 4):
                tail = jnp.where(row4 == r, pltpu.roll(last, 32 * r, 1), tail)
            src[i * 9 + k, 0:4] = low
            src[i * 9 + k, 4:5] = jnp.sum(jnp.where(ends, tail, 0.0), axis=0, keepdims=True)
        return carry

    def build(i, carry):
        for k in range(9):
            for r in range(5):
                taps_row = jnp.broadcast_to(src[i * 9 + k, r : r + 1, :], (32, 128))
                skewed = pltpu.roll(taps_row, 0, 1, stride=1, stride_axis=0)
                keep = lane32 >= row32 if r < 4 else (lane32 & 31) <= row32
                band[i, 32 * k : 32 * k + 32, 128 * r : 128 * r + 128] = jnp.where(keep, skewed, 0.0).astype(BF16)
        return carry

    lax.fori_loop(0, 8, sources, 0)
    lax.fori_loop(0, 8, build, 0)

    def window(layer, i, half, c0, cw):
        x = 32 * half
        low = f[layer, pl.ds(i, 4), x : x + 128, c0 : c0 + cw].reshape(512, cw)
        high = f[layer, pl.ds(i, 4), x + 128 : x + 160, c0 : c0 + cw].reshape(128, cw)
        return jnp.concatenate([low, high], axis=0)

    def mixed(layer, r, columns):
        def row(k):
            return jnp.concatenate([mixf[layer, k : k + 1, lo:hi] for lo, hi in columns], axis=1)

        total = r[0:32] * row(0)
        for k in range(1, 9):
            total += r[32 * k : 32 * k + 32] * row(k)
        return gelu(total).astype(BF16)

    def conv(layer, lo, hi):
        def one(i, carry):
            for half in range(2):
                rows = pl.ds(pl.multiple_of(i * 64 + 32 * half, 32), 32)
                for c0 in (0, 256):
                    r = jnp.dot(band[i], window(layer, i, half, c0, 256), preferred_element_type=F32)
                    act[rows, c0 : c0 + 256] = mixed(layer, r, ((c0, c0 + 256),))
            both = jnp.concatenate([window(layer, i, half, 512, 128) for half in range(2)], axis=1)
            r = jnp.dot(band[i], both, preferred_element_type=F32)
            m = mixed(layer, r, ((512, 640), (512, 640)))
            for half in range(2):
                rows = pl.ds(pl.multiple_of(i * 64 + 32 * half, 32), 32)
                act[rows, 512:640] = m[:, 128 * half : 128 * half + 128]
            return carry

        lax.fori_loop(lo, hi, one, 0)

    def mlp(layer, row, rows):
        hidden = jnp.dot(act[row * 64 : (row + rows) * 64], w1[layer], preferred_element_type=F32)
        hidden = gelu(hidden).astype(BF16)
        update = jnp.dot(hidden, w2[layer], preferred_element_type=F32)
        field = f[layer, row + 2 : row + 2 + rows, own, :].astype(F32)
        result = (field + update.reshape(rows, 64, 640)).astype(BF16)
        if layer == 0:
            f[1, row + 2 : row + 2 + rows, own, :] = result
        else:
            out[row : row + rows] = result

    local["field"].wait()
    arrived(0, "z0")
    begin(0, "sup")
    arrived(0, "p0", "p2", "z2")
    conv(0, 2, 3)
    arrived(0, "p4", "z4")
    conv(0, 3, 4)
    local["in0"].wait()
    local["out0"].wait()
    mlp(0, 2, 2)
    begin(1, "z2", "p2")
    arrived(0, "down", "up")
    begin(0, "fdown", "fup")
    conv(0, 4, 5)
    arrived(0, "p6", "z6")
    begin(0, "sdown")
    conv(0, 5, 6)
    mlp(0, 4, 2)
    begin(1, "z4", "p4")
    arrived(0, "sup", "fup")
    conv(0, 6, 8)
    mlp(0, 6, 2)
    begin(1, "z6", "down", "p6")
    arrived(0, "sdown", "fdown")
    conv(0, 0, 2)
    mlp(0, 0, 2)
    begin(1, "z0", "up", "p0")

    arrived(1, "z6")
    begin(1, "sdown")
    arrived(1, "p2", "p4", "p6", "z2", "z4")
    conv(1, 4, 5)
    arrived(1, "down")
    begin(1, "fdown")
    conv(1, 5, 7)
    arrived(1, "z0")
    begin(1, "sup")
    arrived(1, "p0")
    conv(1, 2, 4)
    arrived(1, "up")
    begin(1, "fup")
    arrived(1, "sdown", "fdown")
    conv(1, 0, 2)
    local["in1"].wait()
    local["out1"].wait()
    mlp(1, 0, 4)
    arrived(1, "sup", "fup")
    conv(1, 7, 8)
    mlp(1, 4, 4)

    for layer in range(2):
        for name in NAMES:
            act_on(layer, name, "sent")


def shards(n_polar, n_azimuth, grid, taps, start, count, mix, w_in, w_out):
    copies = 2 * len(NAMES)
    hbm = pl.BlockSpec(memory_space=pl.ANY)
    return pl.pallas_call(
        functools.partial(body, n_polar, n_azimuth),
        out_shape=jax.ShapeDtypeStruct(grid.shape, grid.dtype),
        in_specs=[hbm] * 7,
        out_specs=pl.BlockSpec(memory_space=pltpu.VMEM),
        scratch_shapes=[
            pltpu.VMEM((2, 11, 192, 640), BF16),
            pltpu.VMEM((8, 288, 640), BF16),
            pltpu.VMEM(w_in.shape, BF16),
            pltpu.VMEM(w_out.shape, BF16),
            pltpu.VMEM(taps.shape, BF16),
            pltpu.SMEM(start.shape, jnp.int32),
            pltpu.SMEM(count.shape, jnp.int32),
            pltpu.VMEM((9, 2, 640), BF16),
            pltpu.VMEM((72, 8, 128), F32),
            pltpu.VMEM((512, 640), BF16),
            pltpu.VMEM((2, 16, 640), F32),
            pltpu.SemaphoreType.DMA((copies,)),
            pltpu.SemaphoreType.DMA((copies,)),
            pltpu.SemaphoreType.DMA((9,)),
        ],
        compiler_params=pltpu.CompilerParams(
            collective_id=0, has_side_effects=True, vmem_limit_bytes=60 * 2**20
        ),
    )(grid, taps, start, count, jnp.transpose(mix, (1, 0, 2)), w_in, w_out)


def solution(mesh):
    return jax.shard_map(
        functools.partial(shards, mesh.shape["polar"], mesh.shape["azimuth"]),
        mesh=mesh,
        in_specs=(
            P("polar", "azimuth", None),
            P("polar", None, None, None),
            P("polar"),
            P("polar"),
            P(),
            P(),
            P(),
        ),
        out_specs=P("polar", "azimuth", None),
        check_vma=False,
    )
```

time: 64.3 us -> 39.4 us (0.61)
  Pallas kernels: 57 us -> 37.3 us
  local copies, waits for them, and re-layouts: 6.81 us -> 1.98 us
    pallas_call x1, Pallas kernels: 57 us -> 37.3 us  [shards(): pl.pallas_call(functools.partial(body, n_polar, n_azimuth), out_shape=jax...]
    unnamed x12 -> x1, local copies, waits for them, and re-layouts: 6.81 us -> 1.98 us
where the time goes in v2:
time: 39.4 us; the launch traced here: 39.3 us
  Pallas kernels  37.3 us (95%)
  local copies, waits for them, and re-layouts  1.98 us (5%)
    pallas_call x1, Pallas kernels, shards(): pl.pallas_call(functools.partial(body, n_polar, n_azimuth), out_shape=jax...  37.3 us
    unnamed x1, local copies, waits for them, and re-layouts  1.98 us

profile of v2, /device:TPU:24, one launch (start us, length us, event | category | flops | bytes accessed | tf_op | source)
XLA Modules:
  0.0 39.3 jit_solution(7353069959694672301)
XLA Ops:
  0.0 37.3 %shard_map.73 = bf16[8,64,640]{2,1,0:T(8,128)(2,1)} custom-call(bf16[8,64,640]{2,1,0:T(8,128)(2,1)} %grid.1, bf16[8,9,4,129]{3,2,1,0:T(4,128)(2,1)} %taps_in.1, s32[8]{0:T(128)} %start_in.1, s32[8]{0:T(128)} %count_in.1, bf16[9,2,640]{2,1,0:T(2,128)(2,1)} %bitcast.1, bf16[2,640,1280]{2,1,0:T(8,128)(2,1)} %w_in.1, bf16[2,1280,640]{2,1,0:T(8,128)(2,1)} %w_out.1), custom_call_target="tpu_custom_call" | custom-call | tf_op jit(solution)/shard_map/pallas_call | solution.py:268
  37.3 2.0 %copy.9 = bf16[8,64,640]{2,1,0:T(8,128)(2,1)} copy(bf16[8,64,640]{2,1,0:T(8,128)(2,1)} %shard_map.73) | data formatting | bytes 1310720

commit v3 on v2

--- a/solution.py
+++ b/solution.py
@@ -11,7 +11,7 @@
 BF16 = jnp.bfloat16
 MESH = pl.DeviceIdType.MESH
 NAMES = (
-    "z0", "z2", "z4", "z6", "p0", "p2", "p4", "p6",
+    "z0", "z1", "z2", "z4", "z6", "p0", "p2", "p4", "p6",
     "down", "up", "sdown", "sup", "fdown", "fup",
 )
 
@@ -23,8 +23,8 @@
 def body(
     n_polar, n_azimuth,
     grid, taps_in, start_in, count_in, mix_in, w_in, w_out, out,
-    f, band, w1, w2, taps, start, count, mix, src, act, mixf,
-    send_sem, recv_sem, local_sem,
+    f, band, w1, w2, taps, start, count, mix, src, act, mixf, res, part,
+    send_sem, recv_sem, local_sem, store_sem,
 ):
     p = lax.axis_index("polar")
     a = lax.axis_index("azimuth")
@@ -50,14 +50,13 @@
         pl.semaphore_signal(barrier, inc=1, device_id=(p + 1, a), device_id_type=MESH)
 
     def field_rows(layer, row, rows):
-        if layer == 0:
-            return grid.at[pl.ds(row, rows)]
         return f.at[layer, pl.ds(row + 2, rows), own]
 
     def transfer(layer, name):
         if name[0] == "z":
             row = int(name[1])
-            return (field_rows(layer, row, 2), f.at[layer, pl.ds(row + 2, 2), core_side], (p, zside), None, None)
+            rows = 1 if row < 2 else 2
+            return (field_rows(layer, row, rows), f.at[layer, pl.ds(row + 2, rows), core_side], (p, zside), None, None)
         if name[0] == "p":
             row = int(name[1])
             return (field_rows(layer, row, 2), f.at[layer, pl.ds(row + 2, 2), chip_side], (p, pair), None, None)
@@ -109,12 +108,15 @@
             ("out1", w_out.at[1], w2.at[1]),
         ))
     }
-    for copy in local.values():
-        copy.start()
+    for name in ("field", "taps", "start", "count", "mix"):
+        local[name].start()
+    local["field"].wait()
 
     pl.semaphore_wait(barrier, 2 + has_low.astype(jnp.int32) + has_high.astype(jnp.int32))
 
-    begin(0, "z0", "down", "up", "p0", "z2", "p2", "z4", "p4", "z6", "p6")
+    begin(0, "z0", "up", "z6", "down", "z4", "p6", "p4", "z2", "p2", "p0", "z1")
+    local["in0"].start()
+    local["out0"].start()
 
     @pl.when(p == 0)
     def _():
@@ -132,12 +134,18 @@
         for k in range(9):
             mixf[layer, k : k + 1] = mix[k, layer : layer + 1].astype(F32)
 
+    even = h == 0
     offset = lax.broadcasted_iota(jnp.int32, (4, 129), 1) - 64
     lane4 = lax.broadcasted_iota(jnp.int32, (4, 128), 1)
     row4 = lax.broadcasted_iota(jnp.int32, (4, 128), 0)
-    lane32 = lax.broadcasted_iota(jnp.int32, (32, 128), 1)
-    row32 = lax.broadcasted_iota(jnp.int32, (32, 128), 0)
-    ends = ((lane4 + 127 - 32 * row4) & 127) >= 96
+    odd4 = row4 & 1
+    lane = lax.broadcasted_iota(jnp.int32, (32, 128), 1)
+    row = lax.broadcasted_iota(jnp.int32, (32, 128), 0)
+    ends3 = ((lane4 - 97 * h - 32 * row4) & 127) < 32
+    ends2 = ((lane4 - 97 * h - 64 * odd4) & 127) < 64
+    keep1 = jnp.where(even, jnp.where(lane >= 96, 0, 64 + row - lane), lane - row)
+    keep3 = jnp.where(even, (lane & 31) - row, row - (lane & 31))
+    keep2 = jnp.where(even, (lane & 63) - row, 32 + row - (lane & 63))
 
     def sources(i, carry):
         inside = (offset >= start[i]) & (offset < start[i] + count[i])
@@ -145,56 +153,107 @@
             v = jnp.where(inside, taps[i, k].astype(F32), 0.0)
             low = v[:, 0:128]
             last = jnp.where(lane4 == 0, jnp.broadcast_to(v[:, 128:129], (4, 128)), low)
-            tail = last
+            third = jnp.where(even, low, last)
+            second = jnp.where(even, low, pltpu.roll(last, 32, 1))
+            rolled = third
             for r in range(1, 4):
-                tail = jnp.where(row4 == r, pltpu.roll(last, 32 * r, 1), tail)
-            src[i * 9 + k, 0:4] = low
-            src[i * 9 + k, 4:5] = jnp.sum(jnp.where(ends, tail, 0.0), axis=0, keepdims=True)
+                rolled = jnp.where(row4 == r, pltpu.roll(third, 32 * r, 1), rolled)
+            pairs = jnp.where(odd4 == 1, pltpu.roll(second, 64, 1), second)
+            src[i * 9 + k, 0:4] = jnp.where(even, pltpu.roll(last, 64, 1), low)
+            src[i * 9 + k, 4:5] = jnp.sum(jnp.where(ends3, rolled, 0.0), axis=0, keepdims=True)
+            src[i * 9 + k, 5:6] = jnp.sum(jnp.where(ends2 & (row4 < 2), pairs, 0.0), axis=0, keepdims=True)
+            src[i * 9 + k, 6:7] = jnp.sum(jnp.where(ends2 & (row4 >= 2), pairs, 0.0), axis=0, keepdims=True)
         return carry
 
     def build(i, carry):
         for k in range(9):
-            for r in range(5):
+            for r in range(7):
                 taps_row = jnp.broadcast_to(src[i * 9 + k, r : r + 1, :], (32, 128))
                 skewed = pltpu.roll(taps_row, 0, 1, stride=1, stride_axis=0)
-                keep = lane32 >= row32 if r < 4 else (lane32 & 31) <= row32
-                band[i, 32 * k : 32 * k + 32, 128 * r : 128 * r + 128] = jnp.where(keep, skewed, 0.0).astype(BF16)
+                keep = keep1 if r < 4 else (keep3 if r == 4 else keep2)
+                band[i, 32 * k : 32 * k + 32, 128 * r : 128 * r + 128] = jnp.where(keep >= 0, skewed, 0.0).astype(BF16)
         return carry
 
     lax.fori_loop(0, 8, sources, 0)
     lax.fori_loop(0, 8, build, 0)
 
-    def window(layer, i, half, c0, cw):
-        x = 32 * half
-        low = f[layer, pl.ds(i, 4), x : x + 128, c0 : c0 + cw].reshape(512, cw)
-        high = f[layer, pl.ds(i, 4), x + 128 : x + 160, c0 : c0 + cw].reshape(128, cw)
-        return jnp.concatenate([low, high], axis=0)
+    def at(x):
+        return pl.multiple_of(x, 32)
+
+    halves = (
+        (at(96 * (1 - h)), at(64 + 32 * h), at(32 + 96 * h), at(32 * (1 - h))),
+        (at(64 - 32 * h), at(32 + 96 * h), at(160 * h), at(32 * h)),
+    )
+
+    def piece(layer, i, x, width, c0, cw):
+        return f[layer, i : i + 4, pl.ds(x, width), c0 : c0 + cw]
+
+    def first_two(layer, i, half, c0, cw):
+        low = piece(layer, i, halves[half][0], 96, c0, cw)
+        high = piece(layer, i, halves[half][1], 32, c0, cw)
+        return jnp.concatenate([low, high], axis=1).reshape(512, cw)
+
+    def third(layer, i, half, c0, cw):
+        return piece(layer, i, halves[half][2], 32, c0, cw).reshape(128, cw)
+
+    def whole(layer, i, half, c0, cw):
+        return jnp.concatenate([first_two(layer, i, half, c0, cw), third(layer, i, half, c0, cw)], axis=0)
+
+    def nearby(layer, i, half, c0, cw):
+        if half == 0:
+            return first_two(layer, i, half, c0, cw)
+        low = piece(layer, i, halves[1][0], 96, c0, cw)
+        return jnp.concatenate([low, jnp.zeros((4, 32, cw), BF16)], axis=1).reshape(512, cw)
 
     def mixed(layer, r, columns):
-        def row(k):
+        def weights(k):
             return jnp.concatenate([mixf[layer, k : k + 1, lo:hi] for lo, hi in columns], axis=1)
 
-        total = r[0:32] * row(0)
+        total = r[0:32] * weights(0)
         for k in range(1, 9):
-            total += r[32 * k : 32 * k + 32] * row(k)
-        return gelu(total).astype(BF16)
-
-    def conv(layer, lo, hi):
-        def one(i, carry):
-            for half in range(2):
-                rows = pl.ds(pl.multiple_of(i * 64 + 32 * half, 32), 32)
-                for c0 in (0, 256):
-                    r = jnp.dot(band[i], window(layer, i, half, c0, 256), preferred_element_type=F32)
-                    act[rows, c0 : c0 + 256] = mixed(layer, r, ((c0, c0 + 256),))
-            both = jnp.concatenate([window(layer, i, half, 512, 128) for half in range(2)], axis=1)
-            r = jnp.dot(band[i], both, preferred_element_type=F32)
-            m = mixed(layer, r, ((512, 640), (512, 640)))
-            for half in range(2):
-                rows = pl.ds(pl.multiple_of(i * 64 + 32 * half, 32), 32)
-                act[rows, 512:640] = m[:, 128 * half : 128 * half + 128]
-            return carry
-
-        lax.fori_loop(lo, hi, one, 0)
+            total += r[32 * k : 32 * k + 32] * weights(k)
+        return total
+
+    def put(i, half, c0, cw, total):
+        rows = pl.ds(pl.multiple_of(i * 64 + halves[half][3], 32), 32)
+        act[rows, c0 : c0 + cw] = gelu(total).astype(BF16)
+
+    def tiles(layer, i, lanes, operand, emit):
+        for half in range(2):
+            for c0 in (0, 256):
+                r = jnp.dot(band[i, :, 0:lanes], operand(layer, i, half, c0, 256), preferred_element_type=F32)
+                emit(i, half, c0, 256, mixed(layer, r, ((c0, c0 + 256),)))
+        both = jnp.concatenate([operand(layer, i, half, 512, 128) for half in range(2)], axis=1)
+        r = jnp.dot(band[i, :, 0:lanes], both, preferred_element_type=F32)
+        total = mixed(layer, r, ((512, 640), (512, 640)))
+        for half in range(2):
+            emit(i, half, 512, 128, total[:, 128 * half : 128 * half + 128])
+
+    def conv(layer, *lats):
+        for i in lats:
+            tiles(layer, i, 640, whole, put)
+
+    def near(layer, *lats):
+        def keep(i, half, c0, cw, total):
+            part[i, 32 * half : 32 * half + 32, c0 : c0 + cw] = total
+
+        for i in lats:
+            tiles(layer, i, 512, nearby, keep)
+
+    def far(layer, *lats):
+        for i in lats:
+            for c0, cw in ((0, 256), (256, 256), (512, 128)):
+                side = f[layer, i : i + 4, chip_side, c0 : c0 + cw].reshape(256, cw)
+                for half, columns, operand in (
+                    (0, slice(512, 640), third(layer, i, 0, c0, cw)),
+                    (1, slice(640, 896), side),
+                ):
+                    r = jnp.dot(band[i, :, columns], operand, preferred_element_type=F32)
+                    before = part[i, 32 * half : 32 * half + 32, c0 : c0 + cw]
+                    put(i, half, c0, cw, before + mixed(layer, r, ((c0, c0 + cw),)))
+
+    def store(row, rows):
+        return pltpu.make_async_copy(res.at[pl.ds(row, rows)], out.at[pl.ds(row, rows)], store_sem.at[row // 2])
 
     def mlp(layer, row, rows):
         hidden = jnp.dot(act[row * 64 : (row + rows) * 64], w1[layer], preferred_element_type=F32)
@@ -205,58 +264,68 @@
         if layer == 0:
             f[1, row + 2 : row + 2 + rows, own, :] = result
         else:
-            out[row : row + rows] = result
-
-    local["field"].wait()
+            res[row : row + rows] = result
+            store(row, rows).start()
+
+    local["in1"].start()
+    local["out1"].start()
+    arrived(0, "p6", "p4", "p2")
+    near(0, 6, 5, 4)
     arrived(0, "z0")
     begin(0, "sup")
-    arrived(0, "p0", "p2", "z2")
-    conv(0, 2, 3)
-    arrived(0, "p4", "z4")
-    conv(0, 3, 4)
+    arrived(0, "p0")
+    near(0, 3, 2)
+    arrived(0, "up")
+    begin(0, "fup")
+    arrived(0, "z6")
+    begin(0, "sdown")
+    arrived(0, "down")
+    begin(0, "fdown")
+    arrived(0, "z4")
+    far(0, 6)
+    arrived(0, "sup", "fup")
+    conv(0, 7)
     local["in0"].wait()
     local["out0"].wait()
+    mlp(0, 6, 2)
+    begin(1, "z6", "down", "p6")
+    arrived(0, "z2")
+    far(0, 4, 5)
+    mlp(0, 4, 2)
+    begin(1, "z4", "p4")
+    arrived(0, "z1")
+    far(0, 2, 3)
     mlp(0, 2, 2)
     begin(1, "z2", "p2")
-    arrived(0, "down", "up")
-    begin(0, "fdown", "fup")
-    conv(0, 4, 5)
-    arrived(0, "p6", "z6")
-    begin(0, "sdown")
-    conv(0, 5, 6)
-    mlp(0, 4, 2)
-    begin(1, "z4", "p4")
-    arrived(0, "sup", "fup")
-    conv(0, 6, 8)
-    mlp(0, 6, 2)
-    begin(1, "z6", "down", "p6")
-    arrived(0, "sdown", "fdown")
-    conv(0, 0, 2)
-    mlp(0, 0, 2)
-    begin(1, "z0", "up", "p0")
-
     arrived(1, "z6")
     begin(1, "sdown")
-    arrived(1, "p2", "p4", "p6", "z2", "z4")
-    conv(1, 4, 5)
     arrived(1, "down")
     begin(1, "fdown")
-    conv(1, 5, 7)
+    arrived(0, "sdown", "fdown")
+    conv(0, 0, 1)
+    mlp(0, 0, 2)
+    begin(1, "z0", "up", "p0", "z1")
+
+    arrived(1, "p4", "p6", "z4")
+    conv(1, 6)
+    arrived(1, "p2", "z2")
+    conv(1, 4, 5)
+    local["in1"].wait()
+    local["out1"].wait()
+    mlp(1, 4, 2)
     arrived(1, "z0")
     begin(1, "sup")
-    arrived(1, "p0")
-    conv(1, 2, 4)
     arrived(1, "up")
     begin(1, "fup")
-    arrived(1, "sdown", "fdown")
-    conv(1, 0, 2)
-    local["in1"].wait()
-    local["out1"].wait()
+    arrived(1, "p0", "z1", "sdown", "fdown")
+    conv(1, 0, 1, 2, 3)
     mlp(1, 0, 4)
     arrived(1, "sup", "fup")
-    conv(1, 7, 8)
-    mlp(1, 4, 4)
-
+    conv(1, 7)
+    mlp(1, 6, 2)
+
+    for row, rows in ((4, 2), (0, 4), (6, 2)):
+        store(row, rows).wait()
     for layer in range(2):
         for name in NAMES:
             act_on(layer, name, "sent")
@@ -269,10 +338,10 @@
         functools.partial(body, n_polar, n_azimuth),
         out_shape=jax.ShapeDtypeStruct(grid.shape, grid.dtype),
         in_specs=[hbm] * 7,
-        out_specs=pl.BlockSpec(memory_space=pltpu.VMEM),
+        out_specs=hbm,
         scratch_shapes=[
             pltpu.VMEM((2, 11, 192, 640), BF16),
-            pltpu.VMEM((8, 288, 640), BF16),
+            pltpu.VMEM((8, 288, 896), BF16),
             pltpu.VMEM(w_in.shape, BF16),
             pltpu.VMEM(w_out.shape, BF16),
             pltpu.VMEM(taps.shape, BF16),
@@ -282,9 +351,12 @@
             pltpu.VMEM((72, 8, 128), F32),
             pltpu.VMEM((512, 640), BF16),
             pltpu.VMEM((2, 16, 640), F32),
+            pltpu.VMEM(grid.shape, BF16),
+            pltpu.VMEM(grid.shape, F32),
             pltpu.SemaphoreType.DMA((copies,)),
             pltpu.SemaphoreType.DMA((copies,)),
             pltpu.SemaphoreType.DMA((9,)),
+            pltpu.SemaphoreType.DMA((4,)),
         ],
         compiler_params=pltpu.CompilerParams(
             collective_id=0, has_side_effects=True, vmem_limit_bytes=60 * 2**20

time: 39.4 us -> 37 us (0.939); the launches traced: 39.3 us -> 36.4 us
  Pallas kernels: 37.3 us -> 34.4 us
    pallas_call x1, Pallas kernels: 37.3 us -> 34.4 us  [shards(): pl.pallas_call(functools.partial(body, n_polar, n_azimuth), out_shape=jax...]
where the time goes in v3:
time: 37 us; the launch traced here: 36.4 us
  Pallas kernels  34.4 us (93%)
  local copies, waits for them, and re-layouts  1.98 us (5%)
    pallas_call x1, Pallas kernels, shards(): pl.pallas_call(functools.partial(body, n_polar, n_azimuth), out_shape=jax...  34.4 us
    unnamed x1, local copies, waits for them, and re-layouts  1.98 us

profile of v3, /device:TPU:24, one launch (start us, length us, event | category | flops | bytes accessed | tf_op | source)
XLA Modules:
  0.0 36.4 jit_solution(4861073603141640081)
XLA Ops:
  0.0 34.4 %shard_map.73 = bf16[8,64,640]{2,1,0:T(8,128)(2,1)} custom-call(bf16[8,64,640]{2,1,0:T(8,128)(2,1)} %grid.1, bf16[8,9,4,129]{3,2,1,0:T(4,128)(2,1)} %taps_in.1, s32[8]{0:T(128)} %start_in.1, s32[8]{0:T(128)} %count_in.1, bf16[9,2,640]{2,1,0:T(2,128)(2,1)} %bitcast.1, bf16[2,640,1280]{2,1,0:T(8,128)(2,1)} %w_in.1, bf16[2,1280,640]{2,1,0:T(8,128)(2,1)} %w_out.1), custom_call_target="tpu_custom_call" | custom-call | tf_op jit(solution)/shard_map/pallas_call | solution.py:337
  34.4 2.0 %copy.9 = bf16[8,64,640]{2,1,0:T(8,128)(2,1)} copy(bf16[8,64,640]{2,1,0:T(8,128)(2,1)} %shard_map.73) | data formatting | bytes 1310720

commit v4 on v3

--- a/solution.py
+++ b/solution.py
@@ -297,28 +297,30 @@
     far(0, 2, 3)
     mlp(0, 2, 2)
     begin(1, "z2", "p2")
+    arrived(0, "sdown", "fdown")
+    conv(0, 0, 1)
     arrived(1, "z6")
     begin(1, "sdown")
+    mlp(0, 0, 2)
+    begin(1, "z0", "up", "p0", "z1")
+
+    arrived(1, "p4", "p6", "z4")
+    conv(1, 6)
     arrived(1, "down")
     begin(1, "fdown")
-    arrived(0, "sdown", "fdown")
-    conv(0, 0, 1)
-    mlp(0, 0, 2)
-    begin(1, "z0", "up", "p0", "z1")
-
-    arrived(1, "p4", "p6", "z4")
-    conv(1, 6)
     arrived(1, "p2", "z2")
     conv(1, 4, 5)
-    local["in1"].wait()
-    local["out1"].wait()
-    mlp(1, 4, 2)
     arrived(1, "z0")
     begin(1, "sup")
     arrived(1, "up")
     begin(1, "fup")
-    arrived(1, "p0", "z1", "sdown", "fdown")
-    conv(1, 0, 1, 2, 3)
+    local["in1"].wait()
+    local["out1"].wait()
+    mlp(1, 4, 2)
+    arrived(1, "p0", "z1")
+    conv(1, 2, 3)
+    arrived(1, "sdown", "fdown")
+    conv(1, 0, 1)
     mlp(1, 0, 4)
     arrived(1, "sup", "fup")
     conv(1, 7)

time: 37 us -> 35.1 us (0.949); the launches traced: 36.4 us -> 34.9 us
  Pallas kernels: 34.4 us -> 32.9 us
    pallas_call x1, Pallas kernels: 34.4 us -> 32.9 us  [shards(): pl.pallas_call(functools.partial(body, n_polar, n_azimuth), out_shape=jax...]
where the time goes in v4:
time: 35.1 us; the launch traced here: 34.9 us
  Pallas kernels  32.9 us (94%)
  local copies, waits for them, and re-layouts  1.98 us (6%)
    pallas_call x1, Pallas kernels, shards(): pl.pallas_call(functools.partial(body, n_polar, n_azimuth), out_shape=jax...  32.9 us
    unnamed x1, local copies, waits for them, and re-layouts  1.98 us

profile of v4, /device:TPU:24, one launch (start us, length us, event | category | flops | bytes accessed | tf_op | source)
XLA Modules:
  0.0 34.9 jit_solution(15979244267319995963)
XLA Ops:
  0.0 32.9 %shard_map.73 = bf16[8,64,640]{2,1,0:T(8,128)(2,1)} custom-call(bf16[8,64,640]{2,1,0:T(8,128)(2,1)} %grid.1, bf16[8,9,4,129]{3,2,1,0:T(4,128)(2,1)} %taps_in.1, s32[8]{0:T(128)} %start_in.1, s32[8]{0:T(128)} %count_in.1, bf16[9,2,640]{2,1,0:T(2,128)(2,1)} %bitcast.1, bf16[2,640,1280]{2,1,0:T(8,128)(2,1)} %w_in.1, bf16[2,1280,640]{2,1,0:T(8,128)(2,1)} %w_out.1), custom_call_target="tpu_custom_call" | custom-call | tf_op jit(solution)/shard_map/pallas_call | solution.py:339
  32.9 2.0 %copy.9 = bf16[8,64,640]{2,1,0:T(8,128)(2,1)} copy(bf16[8,64,640]{2,1,0:T(8,128)(2,1)} %shard_map.73) | data formatting | bytes 1310720

commit v5 on v4

--- a/solution.py
+++ b/solution.py
@@ -306,10 +306,12 @@
 
     arrived(1, "p4", "p6", "z4")
     conv(1, 6)
+    arrived(1, "p2")
+    near(1, 5, 4)
+    arrived(1, "z2")
+    far(1, 4, 5)
     arrived(1, "down")
     begin(1, "fdown")
-    arrived(1, "p2", "z2")
-    conv(1, 4, 5)
     arrived(1, "z0")
     begin(1, "sup")
     arrived(1, "up")

time: 35.1 us -> 34.6 us (0.986)
  Pallas kernels: 32.9 us -> 32.5 us
    pallas_call x1, Pallas kernels: 32.9 us -> 32.5 us  [shards(): pl.pallas_call(functools.partial(body, n_polar, n_azimuth), out_shape=jax...]
where the time goes in v5:
time: 34.6 us; the launch traced here: 34.5 us
  Pallas kernels  32.5 us (94%)
  local copies, waits for them, and re-layouts  1.98 us (6%)
    pallas_call x1, Pallas kernels, shards(): pl.pallas_call(functools.partial(body, n_polar, n_azimuth), out_shape=jax...  32.5 us
    unnamed x1, local copies, waits for them, and re-layouts  1.98 us

profile of v5, /device:TPU:24, one launch (start us, length us, event | category | flops | bytes accessed | tf_op | source)
XLA Modules:
  0.0 34.5 jit_solution(5773490181645481741)
XLA Ops:
  0.0 32.5 %shard_map.73 = bf16[8,64,640]{2,1,0:T(8,128)(2,1)} custom-call(bf16[8,64,640]{2,1,0:T(8,128)(2,1)} %grid.1, bf16[8,9,4,129]{3,2,1,0:T(4,128)(2,1)} %taps_in.1, s32[8]{0:T(128)} %start_in.1, s32[8]{0:T(128)} %count_in.1, bf16[9,2,640]{2,1,0:T(2,128)(2,1)} %bitcast.1, bf16[2,640,1280]{2,1,0:T(8,128)(2,1)} %w_in.1, bf16[2,1280,640]{2,1,0:T(8,128)(2,1)} %w_out.1), custom_call_target="tpu_custom_call" | custom-call | tf_op jit(solution)/shard_map/pallas_call | solution.py:341
  32.5 2.0 %copy.9 = bf16[8,64,640]{2,1,0:T(8,128)(2,1)} copy(bf16[8,64,640]{2,1,0:T(8,128)(2,1)} %shard_map.73) | data formatting | bytes 1310720

commit v6 on v5

--- a/solution.py
+++ b/solution.py
@@ -43,11 +43,13 @@
 
     @pl.when(has_low)
     def _():
-        pl.semaphore_signal(barrier, inc=1, device_id=(p - 1, a), device_id_type=MESH)
+        for peer in (a, zside):
+            pl.semaphore_signal(barrier, inc=1, device_id=(p - 1, peer), device_id_type=MESH)
 
     @pl.when(has_high)
     def _():
-        pl.semaphore_signal(barrier, inc=1, device_id=(p + 1, a), device_id_type=MESH)
+        for peer in (a, zside):
+            pl.semaphore_signal(barrier, inc=1, device_id=(p + 1, peer), device_id_type=MESH)
 
     def field_rows(layer, row, rows):
         return f.at[layer, pl.ds(row + 2, rows), own]
@@ -66,6 +68,8 @@
             return (field_rows(layer, 0, 1), f.at[layer, pl.ds(10, 1), own], (p - 1, a), has_low, has_high)
         if name == "sdown":
             return (f.at[layer, pl.ds(8, 2), chip_side], f.at[layer, pl.ds(0, 2), chip_side], (p + 1, a), has_high, has_low)
+        if name == "sup" and layer == 0:
+            return (field_rows(0, 0, 1), f.at[0, pl.ds(10, 1), core_side], (p - 1, zside), has_low, has_high)
         if name == "sup":
             return (f.at[layer, pl.ds(2, 1), chip_side], f.at[layer, pl.ds(10, 1), chip_side], (p - 1, a), has_low, has_high)
         if name == "fdown":
@@ -112,9 +116,9 @@
         local[name].start()
     local["field"].wait()
 
-    pl.semaphore_wait(barrier, 2 + has_low.astype(jnp.int32) + has_high.astype(jnp.int32))
-
-    begin(0, "z0", "up", "z6", "down", "z4", "p6", "p4", "z2", "p2", "p0", "z1")
+    pl.semaphore_wait(barrier, 2 + 2 * has_low.astype(jnp.int32) + 2 * has_high.astype(jnp.int32))
+
+    begin(0, "sup", "up", "z6", "down", "z4", "p6", "p4", "z2", "p2", "p0", "z0", "z1")
     local["in0"].start()
     local["out0"].start()
 
@@ -271,8 +275,6 @@
     local["out1"].start()
     arrived(0, "p6", "p4", "p2")
     near(0, 6, 5, 4)
-    arrived(0, "z0")
-    begin(0, "sup")
     arrived(0, "p0")
     near(0, 3, 2)
     arrived(0, "up")
@@ -293,7 +295,7 @@
     far(0, 4, 5)
     mlp(0, 4, 2)
     begin(1, "z4", "p4")
-    arrived(0, "z1")
+    arrived(0, "z0", "z1")
     far(0, 2, 3)
     mlp(0, 2, 2)
     begin(1, "z2", "p2")

time: 34.6 us -> 35.6 us (1.029)
  Pallas kernels: 32.5 us -> 33.5 us
    pallas_call x1, Pallas kernels: 32.5 us -> 33.5 us  [shards(): pl.pallas_call(functools.partial(body, n_polar, n_azimuth), out_shape=jax...]
where the time goes in v6:
time: 35.6 us; the launch traced here: 35.5 us
  Pallas kernels  33.5 us (94%)
  local copies, waits for them, and re-layouts  1.98 us (6%)
    pallas_call x1, Pallas kernels, shards(): pl.pallas_call(functools.partial(body, n_polar, n_azimuth), out_shape=jax...  33.5 us
    unnamed x1, local copies, waits for them, and re-layouts  1.98 us

profile of v6, /device:TPU:24, one launch (start us, length us, event | category | flops | bytes accessed | tf_op | source)
XLA Modules:
  0.0 35.5 jit_solution(903400133109762609)
XLA Ops:
  0.0 33.5 %shard_map.73 = bf16[8,64,640]{2,1,0:T(8,128)(2,1)} custom-call(bf16[8,64,640]{2,1,0:T(8,128)(2,1)} %grid.1, bf16[8,9,4,129]{3,2,1,0:T(4,128)(2,1)} %taps_in.1, s32[8]{0:T(128)} %start_in.1, s32[8]{0:T(128)} %count_in.1, bf16[9,2,640]{2,1,0:T(2,128)(2,1)} %bitcast.1, bf16[2,640,1280]{2,1,0:T(8,128)(2,1)} %w_in.1, bf16[2,1280,640]{2,1,0:T(8,128)(2,1)} %w_out.1), custom_call_target="tpu_custom_call" | custom-call | tf_op jit(solution)/shard_map/pallas_call | solution.py:343
  33.5 2.0 %copy.9 = bf16[8,64,640]{2,1,0:T(8,128)(2,1)} copy(bf16[8,64,640]{2,1,0:T(8,128)(2,1)} %shard_map.73) | data formatting | bytes 1310720

commit v7 on v5

--- a/solution.py
+++ b/solution.py
@@ -273,10 +273,10 @@
     near(0, 6, 5, 4)
     arrived(0, "z0")
     begin(0, "sup")
+    arrived(0, "up")
+    begin(0, "fup")
     arrived(0, "p0")
     near(0, 3, 2)
-    arrived(0, "up")
-    begin(0, "fup")
     arrived(0, "z6")
     begin(0, "sdown")
     arrived(0, "down")

time: 34.6 us -> 34.6 us (level)
  no operation moved by 1% of the time
where the time goes in v7:
time: 34.6 us; the launch traced here: 34.5 us
  Pallas kernels  32.5 us (94%)
  local copies, waits for them, and re-layouts  1.98 us (6%)
    pallas_call x1, Pallas kernels, shards(): pl.pallas_call(functools.partial(body, n_polar, n_azimuth), out_shape=jax...  32.5 us
    unnamed x1, local copies, waits for them, and re-layouts  1.98 us

profile of v7, /device:TPU:24, one launch (start us, length us, event | category | flops | bytes accessed | tf_op | source)
XLA Modules:
  0.0 34.5 jit_solution(11509430979555465391)
XLA Ops:
  0.0 32.5 %shard_map.73 = bf16[8,64,640]{2,1,0:T(8,128)(2,1)} custom-call(bf16[8,64,640]{2,1,0:T(8,128)(2,1)} %grid.1, bf16[8,9,4,129]{3,2,1,0:T(4,128)(2,1)} %taps_in.1, s32[8]{0:T(128)} %start_in.1, s32[8]{0:T(128)} %count_in.1, bf16[9,2,640]{2,1,0:T(2,128)(2,1)} %bitcast.1, bf16[2,640,1280]{2,1,0:T(8,128)(2,1)} %w_in.1, bf16[2,1280,640]{2,1,0:T(8,128)(2,1)} %w_out.1), custom_call_target="tpu_custom_call" | custom-call | tf_op jit(solution)/shard_map/pallas_call | solution.py:341
  32.5 2.0 %copy.9 = bf16[8,64,640]{2,1,0:T(8,128)(2,1)} copy(bf16[8,64,640]{2,1,0:T(8,128)(2,1)} %shard_map.73) | data formatting | bytes 1310720

commit v8 on v7

--- a/solution.py
+++ b/solution.py
@@ -281,12 +281,11 @@
     begin(0, "sdown")
     arrived(0, "down")
     begin(0, "fdown")
-    arrived(0, "z4")
-    far(0, 6)
-    arrived(0, "sup", "fup")
-    conv(0, 7)
     local["in0"].wait()
     local["out0"].wait()
+    arrived(0, "z4", "sup", "fup")
+    far(0, 6)
+    conv(0, 7)
     mlp(0, 6, 2)
     begin(1, "z6", "down", "p6")
     arrived(0, "z2")

time: 34.6 us -> 34.6 us (level)
  no operation moved by 1% of the time
where the time goes in v8:
time: 34.6 us; the launch traced here: 34.5 us
  Pallas kernels  32.5 us (94%)
  local copies, waits for them, and re-layouts  1.98 us (6%)
    pallas_call x1, Pallas kernels, shards(): pl.pallas_call(functools.partial(body, n_polar, n_azimuth), out_shape=jax...  32.5 us
    unnamed x1, local copies, waits for them, and re-layouts  1.98 us

profile of v8, /device:TPU:24, one launch (start us, length us, event | category | flops | bytes accessed | tf_op | source)
XLA Modules:
  0.0 34.5 jit_solution(4793674663986055414)
XLA Ops:
  0.0 32.5 %shard_map.73 = bf16[8,64,640]{2,1,0:T(8,128)(2,1)} custom-call(bf16[8,64,640]{2,1,0:T(8,128)(2,1)} %grid.1, bf16[8,9,4,129]{3,2,1,0:T(4,128)(2,1)} %taps_in.1, s32[8]{0:T(128)} %start_in.1, s32[8]{0:T(128)} %count_in.1, bf16[9,2,640]{2,1,0:T(2,128)(2,1)} %bitcast.1, bf16[2,640,1280]{2,1,0:T(8,128)(2,1)} %w_in.1, bf16[2,1280,640]{2,1,0:T(8,128)(2,1)} %w_out.1), custom_call_target="tpu_custom_call" | custom-call | tf_op jit(solution)/shard_map/pallas_call | solution.py:340
  32.5 2.0 %copy.9 = bf16[8,64,640]{2,1,0:T(8,128)(2,1)} copy(bf16[8,64,640]{2,1,0:T(8,128)(2,1)} %shard_map.73) | data formatting | bytes 1310720
